TPU v7x, 32 devices: a whole 2x2x4 slice. The times are simulated.
32 devices in a mesh: tm: 4 (over z), strip: 8 (over y, x, core).
Axes of the slice: x: 2, y: 2, z: 4, core: 2. Of those that a mesh axis runs over, the one named last changes fastest.
Arguments:
- prev_states: float32 [4, 4, 64, 384], P('tm', None, 'strip'), may hold values from -6 to 6
- observation: bfloat16 [4, 64, 384], P(None, 'strip'), may hold values from -6 to 6
- bounds: int32 [5], replicated, may hold values from 0 to 1000, as said below
- coarse_factor: float32 [4, 4], replicated, may hold values from 0 to 1, as said below
- time_weight: float32 [64], replicated, may hold values from -6 to 6
- weight_in: bfloat16 [3, 3, 64, 8], replicated, may hold values from -1 to 1
- weight_mid: bfloat16 [4, 3, 3, 64, 64], replicated, may hold values from -0.375 to 0.375
- weight_out: bfloat16 [3, 3, 4, 64], replicated, may hold values from -0.375 to 0.375
Outputs:
- new_states: float32 [4, 4, 64, 384], P('tm', None, 'strip')
Inputs may be any that keep to these rules, and one draw needn't show every extreme that they name: bounds[0] = 0, bounds[4] = 1000, strictly increasing. `coarse_factor`: every factor lies strictly between 0 and 1.
All inputs are finite; a program needn't handle non-finite values.
Results may differ from a plain program's by a relative error of at most 0.002.
Values may be sent and summed in bfloat16 or wider, within the bound.
A program may use at most 64 MiB of HBM per device.

v0:
```python
import jax
import jax.numpy as jnp
from jax import lax
from jax.sharding import PartitionSpec as P

LAYERS = 6
STEPS = 1000


def extended(block, sides, width):
    for axis, dim in sides:
        count = lax.axis_size(axis)
        forward = [(i, i + 1) for i in range(count - 1)]
        backward = [(target, source) for source, target in forward]
        low = lax.ppermute(
            lax.slice_in_dim(block, block.shape[dim] - width, None, axis=dim), axis, forward
        )
        high = lax.ppermute(lax.slice_in_dim(block, 0, width, axis=dim), axis, backward)
        block = jnp.concatenate([low, block, high], axis=dim)
    return block


def passed_along(shard, axis, by):
    length = lax.axis_size(axis)
    pairs = [(i, i + by) for i in range(length) if 0 <= i + by < length]
    return lax.ppermute(shard, axis, pairs)


def convolve(layer_in, weight):
    rows_out = layer_in.shape[1] - 2
    columns = layer_in.shape[2]
    padded = jnp.pad(layer_in, ((0, 0), (0, 0), (1, 1)))
    summed = jnp.zeros((weight.shape[2], rows_out, columns), jnp.float32)
    for shift_row in range(3):
        for shift_col in range(3):
            window = padded[:, shift_row : shift_row + rows_out, shift_col : shift_col + columns]
            summed = summed + jnp.einsum(
                "oc,crw->orw",
                weight[shift_row, shift_col],
                window,
                preferred_element_type=jnp.float32,
            )
    return summed


def activate(pre_act):
    return jax.nn.silu(pre_act).astype(jnp.bfloat16)


def on_device(
    prev_states, observation, bounds, coarse_factor, time_weight, weight_in, weight_mid, weight_out
):
    slice_index = lax.axis_index("tm")
    start_state = prev_states[0]
    factor = lax.dynamic_index_in_dim(coarse_factor, slice_index, 0, keepdims=False)
    begin = lax.dynamic_index_in_dim(bounds, slice_index, 0, keepdims=False)
    finish = lax.dynamic_index_in_dim(bounds, slice_index + 1, 0, keepdims=False)
    time_now = begin.astype(jnp.float32) / STEPS
    time_step = (finish - begin).astype(jnp.float32) / STEPS
    features = jnp.concatenate([start_state.astype(jnp.bfloat16), observation], axis=0)
    time_bias = time_now * time_weight[:, None, None]
    weights = [weight_in] + [weight_mid[level] for level in range(LAYERS - 2)] + [weight_out]
    velocity = None
    hidden = features
    for level in range(LAYERS):
        padded = extended(hidden, (("strip", 1),), 1)
        pre_act = convolve(padded, weights[level])
        if level == 0:
            pre_act = pre_act + time_bias
        if level == LAYERS - 1:
            velocity = pre_act
        else:
            hidden = activate(pre_act)
    fine = start_state + time_step * velocity
    keeper = (slice_index != 0).astype(jnp.float32)
    jump = fine - keeper * factor[:, None, None] * start_state

    def relay_turn(turn_index, received):
        current = factor[:, None, None] * received + jump
        return passed_along(current, "tm", 1)

    received = lax.fori_loop(0, lax.axis_size("tm") - 1, relay_turn, jnp.zeros_like(jump))
    result = factor[:, None, None] * received + jump
    return result[None]


def solution(mesh):
    placed = (P("tm", None, "strip", None), P(None, "strip", None), P(), P(), P(), P(), P(), P())
    return jax.shard_map(
        on_device,
        mesh=mesh,
        in_specs=placed,
        out_specs=P("tm", None, "strip", None),
        check_vma=False,
    )
```

profile of v0, /device:TPU:28, one launch (start us, length us, event | category | flops | bytes accessed | tf_op | source)
XLA Modules:
  0.0 89.2 jit_solution(3817025996498613239)
XLA Ops:
  0.0 0.8 copy.21
  0.8 0.8 copy.10
  1.6 1.9 %collective-permute-start.1 = (bf16[8,1,384]{2,0,1:T(8,128)(2,1)S(1)}, bf16[8,1,384]{2,0,1:T(8,128)(2,1)S(1)}, u32[]{:S(2)}, u32[]{:S(2)}) collective-permute-start(bf16[8,1,384]{2,0,1:T(8,128)(2,1)S(1)} %get-tuple-element.56), channel_id=1, source_target_pairs={{0,1},{1,2},{2,3},{3,4},{4,5},{5,6},{6,7},{8,9},{9,10},{10,11},{11... | collective-permute-start | bytes 18440 | tf_op jit(solution)/shard_map/ppermute | solution.py:15
  3.5 4.5 %collective-permute-start.2 = (bf16[8,1,384]{2,0,1:T(8,128)(2,1)S(1)}, bf16[8,1,384]{2,0,1:T(8,128)(2,1)S(1)}, u32[]{:S(2)}, u32[]{:S(2)}) collective-permute-start(bf16[8,1,384]{2,0,1:T(8,128)(2,1)S(1)} %get-tuple-element.57), channel_id=1, source_target_pairs={{1,0},{2,1},{3,2},{4,3},{5,4},{6,5},{7,6},{9,8},{10,9},{11,10},{12... | collective-permute-start | bytes 18440 | tf_op jit(solution)/shard_map/ppermute | solution.py:18
  8.1 1.4 %fusion.172 = (s32[1]{0:T(128)}, s32[1]{0:T(128)}) fusion(s32[5]{0:T(128)} %param.12, s32[]{:T(128)S(6)} %select_n.12, s32[]{:T(128)S(6)} %select_n.13), kind=kLoop, calls=%fused_computation.284 | loop fusion | bytes 24 | tf_op jit(solution)/shard_map/jit(dynamic_index_in_dim)/dynamic_slice | solution.py:57
  10.1 0.7 broadcast_multiply_fusion.1
  10.9 1.0 %fusion.106 = f32[8,384,64]{1,2,0:T(8,128)S(1)} fusion(bf16[8,10,386]{2,0,1:T(8,128)(2,1)S(1)} %select_maximum_fusion.2, bf16[3,3,64,8]{2,3,1,0:T(8,128)(2,1)} %param.15), kind=kOutput, calls=%fused_computation.174 | convolution fusion | flops 3145728 | bytes 837632 | tf_op jit(solution)/shard_map/oc,crw->orw/dot_general | solution.py:37
  14.2 0.5 multiply_convert_fusion.4
  14.7 1.9 %collective-permute-start.3 = (bf16[64,1,384]{2,0,1:T(8,128)(2,1)S(1)}, bf16[64,1,384]{2,0,1:T(8,128)(2,1)S(1)}, u32[]{:S(2)}, u32[]{:S(2)}) collective-permute-start(bf16[64,1,384]{2,0,1:T(8,128)(2,1)S(1)} %get-tuple-element.54), channel_id=1, source_target_pairs={{0,1},{1,2},{2,3},{3,4},{4,5},{5,6},{6,7},{8,9},{9,10},{10,11},{11... | collective-permute-start | bytes 147464 | tf_op jit(solution)/shard_map/ppermute | solution.py:15
  16.6 4.5 %collective-permute-start.4 = (bf16[64,1,384]{2,0,1:T(8,128)(2,1)S(1)}, bf16[64,1,384]{2,0,1:T(8,128)(2,1)S(1)}, u32[]{:S(2)}, u32[]{:S(2)}) collective-permute-start(bf16[64,1,384]{2,0,1:T(8,128)(2,1)S(1)} %get-tuple-element.55), channel_id=1, source_target_pairs={{1,0},{2,1},{3,2},{4,3},{5,4},{6,5},{7,6},{9,8},{10,9},{11,10},{12... | collective-permute-start | bytes 147464 | tf_op jit(solution)/shard_map/ppermute | solution.py:18
  21.2 1.7 %collective-permute-done.4 = bf16[64,1,384]{2,0,1:T(8,128)(2,1)S(1)} collective-permute-done((bf16[64,1,384]{2,0,1:T(8,128)(2,1)S(1)}, bf16[64,1,384]{2,0,1:T(8,128)(2,1)S(1)}, u32[]{:S(2)}, u32[]{:S(2)}) %collective-permute-start.4) | collective-permute-done | bytes 49184 | tf_op jit(solution)/shard_map/ppermute | solution.py:18
  25.4 0.4 multiply_convert_fusion.3
  25.8 1.9 %collective-permute-start.5 = (bf16[64,1,384]{2,0,1:T(8,128)(2,1)S(1)}, bf16[64,1,384]{2,0,1:T(8,128)(2,1)S(1)}, u32[]{:S(2)}, u32[]{:S(2)}) collective-permute-start(bf16[64,1,384]{2,0,1:T(8,128)(2,1)S(1)} %get-tuple-element.52), channel_id=1, source_target_pairs={{0,1},{1,2},{2,3},{3,4},{4,5},{5,6},{6,7},{8,9},{9,10},{10,11},{11... | collective-permute-start | bytes 147464 | tf_op jit(solution)/shard_map/ppermute | solution.py:15
  27.7 4.6 %collective-permute-start.6 = (bf16[64,1,384]{2,0,1:T(8,128)(2,1)S(1)}, bf16[64,1,384]{2,0,1:T(8,128)(2,1)S(1)}, u32[]{:S(2)}, u32[]{:S(2)}) collective-permute-start(bf16[64,1,384]{2,0,1:T(8,128)(2,1)S(1)} %get-tuple-element.53), channel_id=1, source_target_pairs={{1,0},{2,1},{3,2},{4,3},{5,4},{6,5},{7,6},{9,8},{10,9},{11,10},{12... | collective-permute-start | bytes 147464 | tf_op jit(solution)/shard_map/ppermute | solution.py:18
  32.3 1.7 %collective-permute-done.6 = bf16[64,1,384]{2,0,1:T(8,128)(2,1)S(1)} collective-permute-done((bf16[64,1,384]{2,0,1:T(8,128)(2,1)S(1)}, bf16[64,1,384]{2,0,1:T(8,128)(2,1)S(1)}, u32[]{:S(2)}, u32[]{:S(2)}) %collective-permute-start.6) | collective-permute-done | bytes 49184 | tf_op jit(solution)/shard_map/ppermute | solution.py:18
  37.0 1.9 %collective-permute-start.7 = (bf16[64,1,384]{2,0,1:T(8,128)(2,1)S(1)}, bf16[64,1,384]{2,0,1:T(8,128)(2,1)S(1)}, u32[]{:S(2)}, u32[]{:S(2)}) collective-permute-start(bf16[64,1,384]{2,0,1:T(8,128)(2,1)S(1)} %get-tuple-element.50), channel_id=1, source_target_pairs={{0,1},{1,2},{2,3},{3,4},{4,5},{5,6},{6,7},{8,9},{9,10},{10,11},{11... | collective-permute-start | bytes 147464 | tf_op jit(solution)/shard_map/ppermute | solution.py:15
  38.9 4.6 %collective-permute-start.8 = (bf16[64,1,384]{2,0,1:T(8,128)(2,1)S(1)}, bf16[64,1,384]{2,0,1:T(8,128)(2,1)S(1)}, u32[]{:S(2)}, u32[]{:S(2)}) collective-permute-start(bf16[64,1,384]{2,0,1:T(8,128)(2,1)S(1)} %get-tuple-element.51), channel_id=1, source_target_pairs={{1,0},{2,1},{3,2},{4,3},{5,4},{6,5},{7,6},{9,8},{10,9},{11,10},{12... | collective-permute-start | bytes 147464 | tf_op jit(solution)/shard_map/ppermute | solution.py:18
  43.5 1.7 %collective-permute-done.8 = bf16[64,1,384]{2,0,1:T(8,128)(2,1)S(1)} collective-permute-done((bf16[64,1,384]{2,0,1:T(8,128)(2,1)S(1)}, bf16[64,1,384]{2,0,1:T(8,128)(2,1)S(1)}, u32[]{:S(2)}, u32[]{:S(2)}) %collective-permute-start.8) | collective-permute-done | bytes 49184 | tf_op jit(solution)/shard_map/ppermute | solution.py:18
  48.2 1.9 %collective-permute-start.9 = (bf16[64,1,384]{2,0,1:T(8,128)(2,1)S(1)}, bf16[64,1,384]{2,0,1:T(8,128)(2,1)S(1)}, u32[]{:S(2)}, u32[]{:S(2)}) collective-permute-start(bf16[64,1,384]{2,0,1:T(8,128)(2,1)S(1)} %get-tuple-element.48), channel_id=1, source_target_pairs={{0,1},{1,2},{2,3},{3,4},{4,5},{5,6},{6,7},{8,9},{9,10},{10,11},{11... | collective-permute-start | bytes 147464 | tf_op jit(solution)/shard_map/ppermute | solution.py:15
  50.1 4.6 %collective-permute-start.10 = (bf16[64,1,384]{2,0,1:T(8,128)(2,1)S(1)}, bf16[64,1,384]{2,0,1:T(8,128)(2,1)S(1)}, u32[]{:S(2)}, u32[]{:S(2)}) collective-permute-start(bf16[64,1,384]{2,0,1:T(8,128)(2,1)S(1)} %get-tuple-element.49), channel_id=1, source_target_pairs={{1,0},{2,1},{3,2},{4,3},{5,4},{6,5},{7,6},{9,8},{10,9},{11,10},{12... | collective-permute-start | bytes 147464 | tf_op jit(solution)/shard_map/ppermute | solution.py:18
  54.7 1.7 %collective-permute-done.10 = bf16[64,1,384]{2,0,1:T(8,128)(2,1)S(1)} collective-permute-done((bf16[64,1,384]{2,0,1:T(8,128)(2,1)S(1)}, bf16[64,1,384]{2,0,1:T(8,128)(2,1)S(1)}, u32[]{:S(2)}, u32[]{:S(2)}) %collective-permute-start.10) | collective-permute-done | bytes 49184 | tf_op jit(solution)/shard_map/ppermute | solution.py:18
  59.4 1.9 %collective-permute-start.11 = (bf16[64,1,384]{2,0,1:T(8,128)(2,1)S(1)}, bf16[64,1,384]{2,0,1:T(8,128)(2,1)S(1)}, u32[]{:S(2)}, u32[]{:S(2)}) collective-permute-start(bf16[64,1,384]{2,0,1:T(8,128)(2,1)S(1)} %get-tuple-element.46), channel_id=1, source_target_pairs={{0,1},{1,2},{2,3},{3,4},{4,5},{5,6},{6,7},{8,9},{9,10},{10,11},{11... | collective-permute-start | bytes 147464 | tf_op jit(solution)/shard_map/ppermute | solution.py:15
  61.3 4.6 %collective-permute-start.12 = (bf16[64,1,384]{2,0,1:T(8,128)(2,1)S(1)}, bf16[64,1,384]{2,0,1:T(8,128)(2,1)S(1)}, u32[]{:S(2)}, u32[]{:S(2)}) collective-permute-start(bf16[64,1,384]{2,0,1:T(8,128)(2,1)S(1)} %get-tuple-element.47), channel_id=1, source_target_pairs={{1,0},{2,1},{3,2},{4,3},{5,4},{6,5},{7,6},{9,8},{10,9},{11,10},{12... | collective-permute-start | bytes 147464 | tf_op jit(solution)/shard_map/ppermute | solution.py:18
  65.9 0.7 broadcast_multiply_fusion
  70.3 18.2 %while.10 = (s32[]{:T(128)}, f32[4,8,384]{2,1,0:T(8,128)S(1)}, f32[4]{0:T(128)S(1)}, f32[4,8,384]{2,1,0:T(8,128)S(1)}, s32[]{:T(128)}) while((s32[]{:T(128)}, f32[4,8,384]{2,1,0:T(8,128)S(1)}, f32[4]{0:T(128)S(1)}, f32[4,8,384]{2,1,0:T(8,128)S(1)}, s32[]{:T(128)}) %tuple.30), condition=%wide.region_1.2_spmd, body=%wide.region_0.1_spmd.sunk | while | flops 24578 | bytes 344181 | solution.py:82
  70.4 1.3 %collective-permute-start = (f32[4,8,384]{2,1,0:T(8,128)S(1)}, f32[4,8,384]{2,1,0:T(8,128)S(1)}, u32[]{:S(2)}, u32[]{:S(2)}) collective-permute-start(f32[4,8,384]{2,1,0:T(8,128)S(1)} %multiply_add_fusion.2), channel_id=1, source_target_pairs={{0,8},{8,16},{16,24},{1,9},{9,17},{17,25},{2,10},{10,18},{18,26},{... | collective-permute-start | bytes 147464 | tf_op jit(solution)/shard_map/while/body/eval_jaxpr/ppermute | solution.py:26
  71.7 4.7 %collective-permute-done = f32[4,8,384]{2,1,0:T(8,128)S(1)} collective-permute-done((f32[4,8,384]{2,1,0:T(8,128)S(1)}, f32[4,8,384]{2,1,0:T(8,128)S(1)}, u32[]{:S(2)}, u32[]{:S(2)}) %collective-permute-start) | collective-permute-done | bytes 49184 | tf_op jit(solution)/shard_map/while/body/eval_jaxpr/ppermute | solution.py:26
  76.4 1.3 %collective-permute-start = (f32[4,8,384]{2,1,0:T(8,128)S(1)}, f32[4,8,384]{2,1,0:T(8,128)S(1)}, u32[]{:S(2)}, u32[]{:S(2)}) collective-permute-start(f32[4,8,384]{2,1,0:T(8,128)S(1)} %multiply_add_fusion.2), channel_id=1, source_target_pairs={{0,8},{8,16},{16,24},{1,9},{9,17},{17,25},{2,10},{10,18},{18,26},{... | collective-permute-start | bytes 147464 | tf_op jit(solution)/shard_map/while/body/eval_jaxpr/ppermute | solution.py:26
  77.7 4.7 %collective-permute-done = f32[4,8,384]{2,1,0:T(8,128)S(1)} collective-permute-done((f32[4,8,384]{2,1,0:T(8,128)S(1)}, f32[4,8,384]{2,1,0:T(8,128)S(1)}, u32[]{:S(2)}, u32[]{:S(2)}) %collective-permute-start) | collective-permute-done | bytes 49184 | tf_op jit(solution)/shard_map/while/body/eval_jaxpr/ppermute | solution.py:26
  82.5 1.3 %collective-permute-start = (f32[4,8,384]{2,1,0:T(8,128)S(1)}, f32[4,8,384]{2,1,0:T(8,128)S(1)}, u32[]{:S(2)}, u32[]{:S(2)}) collective-permute-start(f32[4,8,384]{2,1,0:T(8,128)S(1)} %multiply_add_fusion.2), channel_id=1, source_target_pairs={{0,8},{8,16},{16,24},{1,9},{9,17},{17,25},{2,10},{10,18},{18,26},{... | collective-permute-start | bytes 147464 | tf_op jit(solution)/shard_map/while/body/eval_jaxpr/ppermute | solution.py:26
  83.8 4.7 %collective-permute-done = f32[4,8,384]{2,1,0:T(8,128)S(1)} collective-permute-done((f32[4,8,384]{2,1,0:T(8,128)S(1)}, f32[4,8,384]{2,1,0:T(8,128)S(1)}, u32[]{:S(2)}, u32[]{:S(2)}) %collective-permute-start) | collective-permute-done | bytes 49184 | tf_op jit(solution)/shard_map/while/body/eval_jaxpr/ppermute | solution.py:26
  88.5 0.6 copy.13
  (86 shorter events, 16.2 us)
Async XLA Ops:
  0.0 11.9 %copy-start.2 = (bf16[3,3,64,8]{2,3,1,0:T(8,128)(2,1)S(1)}, bf16[3,3,64,8]{2,3,1,0:T(8,128)(2,1)}, u32[]{:S(2)}) copy-start(bf16[3,3,64,8]{2,3,1,0:T(8,128)(2,1)} %param.15) | copy-start | bytes 27652
  1.6 9.2 %collective-permute-start.1 = (bf16[8,1,384]{2,0,1:T(8,128)(2,1)S(1)}, bf16[8,1,384]{2,0,1:T(8,128)(2,1)S(1)}, u32[]{:S(2)}, u32[]{:S(2)}) collective-permute-start(bf16[8,1,384]{2,0,1:T(8,128)(2,1)S(1)} %get-tuple-element.56), channel_id=1, source_target_pairs={{0,1},{1,2},{2,3},{3,4},{4,5},{5,6},{6,7},{8,9},{9,10},{10,11},{11... | collective-permute-start | bytes 18440 | tf_op jit(solution)/shard_map/ppermute | solution.py:15
  3.5 7.3 %collective-permute-start.2 = (bf16[8,1,384]{2,0,1:T(8,128)(2,1)S(1)}, bf16[8,1,384]{2,0,1:T(8,128)(2,1)S(1)}, u32[]{:S(2)}, u32[]{:S(2)}) collective-permute-start(bf16[8,1,384]{2,0,1:T(8,128)(2,1)S(1)} %get-tuple-element.57), channel_id=1, source_target_pairs={{1,0},{2,1},{3,2},{4,3},{5,4},{6,5},{7,6},{9,8},{10,9},{11,10},{12... | collective-permute-start | bytes 18440 | tf_op jit(solution)/shard_map/ppermute | solution.py:18
  14.2 7.0 %copy-start = (bf16[4,3,3,64,64]{4,3,2,1,0:T(8,128)(2,1)S(1)}, bf16[4,3,3,64,64]{4,3,2,1,0:T(8,128)(2,1)}, u32[]{:S(2)}) copy-start(bf16[4,3,3,64,64]{4,3,2,1,0:T(8,128)(2,1)} %param.16) | copy-start | bytes 884740
  14.7 6.5 %collective-permute-start.3 = (bf16[64,1,384]{2,0,1:T(8,128)(2,1)S(1)}, bf16[64,1,384]{2,0,1:T(8,128)(2,1)S(1)}, u32[]{:S(2)}, u32[]{:S(2)}) collective-permute-start(bf16[64,1,384]{2,0,1:T(8,128)(2,1)S(1)} %get-tuple-element.54), channel_id=1, source_target_pairs={{0,1},{1,2},{2,3},{3,4},{4,5},{5,6},{6,7},{8,9},{9,10},{10,11},{11... | collective-permute-start | bytes 147464 | tf_op jit(solution)/shard_map/ppermute | solution.py:15
  16.6 6.3 %collective-permute-start.4 = (bf16[64,1,384]{2,0,1:T(8,128)(2,1)S(1)}, bf16[64,1,384]{2,0,1:T(8,128)(2,1)S(1)}, u32[]{:S(2)}, u32[]{:S(2)}) collective-permute-start(bf16[64,1,384]{2,0,1:T(8,128)(2,1)S(1)} %get-tuple-element.55), channel_id=1, source_target_pairs={{1,0},{2,1},{3,2},{4,3},{5,4},{6,5},{7,6},{9,8},{10,9},{11,10},{12... | collective-permute-start | bytes 147464 | tf_op jit(solution)/shard_map/ppermute | solution.py:18
  25.8 6.5 %collective-permute-start.5 = (bf16[64,1,384]{2,0,1:T(8,128)(2,1)S(1)}, bf16[64,1,384]{2,0,1:T(8,128)(2,1)S(1)}, u32[]{:S(2)}, u32[]{:S(2)}) collective-permute-start(bf16[64,1,384]{2,0,1:T(8,128)(2,1)S(1)} %get-tuple-element.52), channel_id=1, source_target_pairs={{0,1},{1,2},{2,3},{3,4},{4,5},{5,6},{6,7},{8,9},{9,10},{10,11},{11... | collective-permute-start | bytes 147464 | tf_op jit(solution)/shard_map/ppermute | solution.py:15
  27.7 6.3 %collective-permute-start.6 = (bf16[64,1,384]{2,0,1:T(8,128)(2,1)S(1)}, bf16[64,1,384]{2,0,1:T(8,128)(2,1)S(1)}, u32[]{:S(2)}, u32[]{:S(2)}) collective-permute-start(bf16[64,1,384]{2,0,1:T(8,128)(2,1)S(1)} %get-tuple-element.53), channel_id=1, source_target_pairs={{1,0},{2,1},{3,2},{4,3},{5,4},{6,5},{7,6},{9,8},{10,9},{11,10},{12... | collective-permute-start | bytes 147464 | tf_op jit(solution)/shard_map/ppermute | solution.py:18
  37.0 6.5 %collective-permute-start.7 = (bf16[64,1,384]{2,0,1:T(8,128)(2,1)S(1)}, bf16[64,1,384]{2,0,1:T(8,128)(2,1)S(1)}, u32[]{:S(2)}, u32[]{:S(2)}) collective-permute-start(bf16[64,1,384]{2,0,1:T(8,128)(2,1)S(1)} %get-tuple-element.50), channel_id=1, source_target_pairs={{0,1},{1,2},{2,3},{3,4},{4,5},{5,6},{6,7},{8,9},{9,10},{10,11},{11... | collective-permute-start | bytes 147464 | tf_op jit(solution)/shard_map/ppermute | solution.py:15
  38.9 6.3 %collective-permute-start.8 = (bf16[64,1,384]{2,0,1:T(8,128)(2,1)S(1)}, bf16[64,1,384]{2,0,1:T(8,128)(2,1)S(1)}, u32[]{:S(2)}, u32[]{:S(2)}) collective-permute-start(bf16[64,1,384]{2,0,1:T(8,128)(2,1)S(1)} %get-tuple-element.51), channel_id=1, source_target_pairs={{1,0},{2,1},{3,2},{4,3},{5,4},{6,5},{7,6},{9,8},{10,9},{11,10},{12... | collective-permute-start | bytes 147464 | tf_op jit(solution)/shard_map/ppermute | solution.py:18
  48.2 6.5 %collective-permute-start.9 = (bf16[64,1,384]{2,0,1:T(8,128)(2,1)S(1)}, bf16[64,1,384]{2,0,1:T(8,128)(2,1)S(1)}, u32[]{:S(2)}, u32[]{:S(2)}) collective-permute-start(bf16[64,1,384]{2,0,1:T(8,128)(2,1)S(1)} %get-tuple-element.48), channel_id=1, source_target_pairs={{0,1},{1,2},{2,3},{3,4},{4,5},{5,6},{6,7},{8,9},{9,10},{10,11},{11... | collective-permute-start | bytes 147464 | tf_op jit(solution)/shard_map/ppermute | solution.py:15
  50.1 6.3 %collective-permute-start.10 = (bf16[64,1,384]{2,0,1:T(8,128)(2,1)S(1)}, bf16[64,1,384]{2,0,1:T(8,128)(2,1)S(1)}, u32[]{:S(2)}, u32[]{:S(2)}) collective-permute-start(bf16[64,1,384]{2,0,1:T(8,128)(2,1)S(1)} %get-tuple-element.49), channel_id=1, source_target_pairs={{1,0},{2,1},{3,2},{4,3},{5,4},{6,5},{7,6},{9,8},{10,9},{11,10},{12... | collective-permute-start | bytes 147464 | tf_op jit(solution)/shard_map/ppermute | solution.py:18
  59.3 8.8 %copy-start.3 = (bf16[3,3,4,64]{3,2,1,0:T(4,128)(2,1)S(1)}, bf16[3,3,4,64]{3,2,1,0:T(4,128)(2,1)}, u32[]{:S(2)}) copy-start(bf16[3,3,4,64]{3,2,1,0:T(4,128)(2,1)} %param.17) | copy-start | bytes 13828
  59.4 8.5 %collective-permute-start.11 = (bf16[64,1,384]{2,0,1:T(8,128)(2,1)S(1)}, bf16[64,1,384]{2,0,1:T(8,128)(2,1)S(1)}, u32[]{:S(2)}, u32[]{:S(2)}) collective-permute-start(bf16[64,1,384]{2,0,1:T(8,128)(2,1)S(1)} %get-tuple-element.46), channel_id=1, source_target_pairs={{0,1},{1,2},{2,3},{3,4},{4,5},{5,6},{6,7},{8,9},{9,10},{10,11},{11... | collective-permute-start | bytes 147464 | tf_op jit(solution)/shard_map/ppermute | solution.py:15
  61.3 6.5 %collective-permute-start.12 = (bf16[64,1,384]{2,0,1:T(8,128)(2,1)S(1)}, bf16[64,1,384]{2,0,1:T(8,128)(2,1)S(1)}, u32[]{:S(2)}, u32[]{:S(2)}) collective-permute-start(bf16[64,1,384]{2,0,1:T(8,128)(2,1)S(1)} %get-tuple-element.47), channel_id=1, source_target_pairs={{1,0},{2,1},{3,2},{4,3},{5,4},{6,5},{7,6},{9,8},{10,9},{11,10},{12... | collective-permute-start | bytes 147464 | tf_op jit(solution)/shard_map/ppermute | solution.py:18
  69.3 0.8 copy-start.1
  70.4 6.0 %collective-permute-start = (f32[4,8,384]{2,1,0:T(8,128)S(1)}, f32[4,8,384]{2,1,0:T(8,128)S(1)}, u32[]{:S(2)}, u32[]{:S(2)}) collective-permute-start(f32[4,8,384]{2,1,0:T(8,128)S(1)} %multiply_add_fusion.2), channel_id=1, source_target_pairs={{0,8},{8,16},{16,24},{1,9},{9,17},{17,25},{2,10},{10,18},{18,26},{... | collective-permute-start | bytes 147464 | tf_op jit(solution)/shard_map/while/body/eval_jaxpr/ppermute | solution.py:26
  76.4 6.0 %collective-permute-start = (f32[4,8,384]{2,1,0:T(8,128)S(1)}, f32[4,8,384]{2,1,0:T(8,128)S(1)}, u32[]{:S(2)}, u32[]{:S(2)}) collective-permute-start(f32[4,8,384]{2,1,0:T(8,128)S(1)} %multiply_add_fusion.2), channel_id=1, source_target_pairs={{0,8},{8,16},{16,24},{1,9},{9,17},{17,25},{2,10},{10,18},{18,26},{... | collective-permute-start | bytes 147464 | tf_op jit(solution)/shard_map/while/body/eval_jaxpr/ppermute | solution.py:26
  82.5 6.0 %collective-permute-start = (f32[4,8,384]{2,1,0:T(8,128)S(1)}, f32[4,8,384]{2,1,0:T(8,128)S(1)}, u32[]{:S(2)}, u32[]{:S(2)}) collective-permute-start(f32[4,8,384]{2,1,0:T(8,128)S(1)} %multiply_add_fusion.2), channel_id=1, source_target_pairs={{0,8},{8,16},{16,24},{1,9},{9,17},{17,25},{2,10},{10,18},{18,26},{... | collective-permute-start | bytes 147464 | tf_op jit(solution)/shard_map/while/body/eval_jaxpr/ppermute | solution.py:26
where the time goes:
time: 89.9 us; the launch traced here: 89.2 us
  starting transfers between devices  42.7 us (47%)
  waiting for transfers between devices  20.9 us (23%)
  matrix products  15.7 us (17%)
  local copies, waits for them, and re-layouts  3.86 us (4%)
  other arithmetic  3.35 us (4%)
  between operations  2.55 us (3%)
    ppermute x6, starting transfers between devices, extended(): lax.ppermute(lax.slice_in_dim(block, 0, width, axis=dim), axis, backward)  27.4 us
    dot_general x54, matrix products, convolve(): jnp.einsum('oc,crw->orw', weight[shift_row, shift_col], window, preferred...  15.7 us
    ppermute x3, waiting for transfers between devices, passed_along(): return lax.ppermute(shard, axis, pairs)  14 us
    ppermute x6, starting transfers between devices, extended(): lax.ppermute(lax.slice_in_dim(block, block.shape[dim] - width, None, axis...  11.5 us
    ppermute x6, waiting for transfers between devices, extended(): lax.ppermute(lax.slice_in_dim(block, 0, width, axis=dim), axis, backward)  6.82 us
    ppermute x3, starting transfers between devices, passed_along(): return lax.ppermute(shard, axis, pairs)  3.84 us
  transfers between devices with their start and end apart: 15, of which 7 were waited for; matrix products, arithmetic and copies ran while one was open for 3% of the time, Pallas kernels for 0%

commit v1 on v0

v1 whole, which is shorter than its diff:
```python
import functools

import jax
import jax.numpy as jnp
from jax import lax
from jax.experimental import pallas as pl
from jax.experimental.pallas import tpu as pltpu
from jax.sharding import PartitionSpec as P

STEPS = 1000
MESH = pl.DeviceIdType.MESH
F32 = jnp.float32
BF16 = jnp.bfloat16


def kernel(
    slices,
    strips,
    prev_ref,
    obs_ref,
    bounds_ref,
    factor_ref,
    time_ref,
    win_ref,
    wmid_ref,
    wout_ref,
    out_ref,
    own,
    above,
    below,
    field,
    w_first,
    w_mid,
    w_last,
    hidden_a,
    hidden_b,
    arrived,
    halo_send,
    halo_recv,
    relay_send,
    relay_recv,
):
    t = lax.axis_index("tm")
    s = lax.axis_index("strip")
    channels, rows, cols = prev_ref.shape[1:]
    hid = time_ref.shape[1]
    middle = wmid_ref.shape[0]
    not_top, not_bottom = s > 0, s < strips - 1
    not_first, not_last = t > 0, t < slices - 1

    barrier = pltpu.get_barrier_semaphore()

    def greet(tt, ss):
        pl.semaphore_signal(barrier, inc=1, device_id=(tt, ss), device_id_type=MESH)

    pl.when(not_top)(lambda: greet(t, s - 1))
    pl.when(not_bottom)(lambda: greet(t, s + 1))
    pl.when(not_first)(lambda: greet(t - 1, s))
    pl.when(not_last)(lambda: greet(t + 1, s))

    for c in range(channels):
        field[c, rows : 2 * rows, :] = prev_ref[0, c]
        field[channels + c, rows : 2 * rows, :] = obs_ref[c].astype(F32)
    own[...] = field[:, rows : 2 * rows, :].reshape(2 * channels * rows, cols).astype(BF16)

    greeted = (
        not_top.astype(jnp.int32)
        + not_bottom.astype(jnp.int32)
        + not_first.astype(jnp.int32)
        + not_last.astype(jnp.int32)
    )
    pl.semaphore_wait(barrier, greeted)

    def to_above():
        return pltpu.make_async_remote_copy(
            own, below, halo_send.at[0], halo_recv.at[1], (t, s - 1), MESH
        )

    def to_below():
        return pltpu.make_async_remote_copy(
            own, above, halo_send.at[1], halo_recv.at[0], (t, s + 1), MESH
        )

    pl.when(not_top)(lambda: to_above().start())
    pl.when(not_bottom)(lambda: to_below().start())

    lane = lax.broadcasted_iota(jnp.int32, (2 * channels, 256), 1)
    chan = lax.broadcasted_iota(jnp.int32, (2 * channels, 256), 0)
    base = jnp.zeros((hid, 256), F32)
    for i in range(3):
        for j in range(3):
            pick = (lane == j * 64 + chan * 8 + i).astype(F32).astype(BF16)
            base = base + jnp.dot(win_ref[i, j], pick, preferred_element_type=F32)
    base = base * 0.5
    for b in range(6):
        turned = pltpu.roll(base, b, 1) if b else base
        w_first[b * hid : (b + 1) * hid, :] = turned.astype(BF16)

    half = jnp.asarray(0.5, BF16)
    none = jnp.zeros((hid, hid), BF16)
    for level in range(middle):
        for j in range(3):
            w = [wmid_ref[level, i, j] * half for i in range(3)]
            at = 2 * j * hid
            w_mid[level, at : at + hid, :] = jnp.concatenate(w + [none], axis=1)
            w_mid[level, at + hid : at + 2 * hid, :] = jnp.concatenate([none] + w, axis=1)

    block = lax.broadcasted_iota(jnp.int32, (rows, 128), 1) // hid
    row_at = lax.broadcasted_iota(jnp.int32, (rows, 128), 0)
    for j in range(3):
        taps = []
        for i in range(3):
            tap = wout_ref[i, j].astype(F32)
            taps.append(jnp.concatenate([tap, tap], axis=1))
        for tile in range((rows + 2) * hid // 128):
            diff = block + 2 * tile - row_at
            parts = []
            for o in range(channels):
                part = jnp.zeros((rows, 128), F32)
                for i in range(3):
                    spread = jnp.broadcast_to(taps[i][o : o + 1], (rows, 128))
                    part = jnp.where(diff == i, spread, part)
                parts.append(part)
            w_last[
                j * channels * rows : (j + 1) * channels * rows, tile * 128 : (tile + 1) * 128
            ] = jnp.concatenate(parts, axis=0).astype(BF16)

    begin = bounds_ref[t].astype(F32)
    finish = bounds_ref[t + 1].astype(F32)
    time_now = begin / STEPS
    time_step = (finish - begin) / STEPS
    eye = lax.broadcasted_iota(jnp.int32, (hid, hid), 0) == lax.broadcasted_iota(
        jnp.int32, (hid, hid), 1
    )
    spread = jnp.broadcast_to(time_ref[...], (hid, hid))
    column = jnp.sum(jnp.where(eye, spread, 0.0), axis=1, keepdims=True)
    bias = (0.5 * time_now) * column

    keep_top = not_top.astype(F32)
    keep_bottom = not_bottom.astype(F32)

    def activated(u, row):
        h = u + u * jnp.tanh(u)
        if row < rows:
            h = h * keep_top
        elif row >= 2 * rows:
            h = h * keep_bottom
        return h.astype(BF16)

    def from_left(v):
        at = lax.broadcasted_iota(jnp.int32, v.shape, 1)
        return jnp.where(at == 0, 0.0, pltpu.roll(v, 1, 1))

    def from_right(v):
        at = lax.broadcasted_iota(jnp.int32, v.shape, 1)
        return jnp.where(at == cols - 1, 0.0, pltpu.roll(v, cols - 1, 1))

    def first_layer(group):
        start = 2 + 6 * group
        window = field[:, start : start + 8, :].reshape(16 * channels, cols)
        stacked = jnp.concatenate(
            [from_left(window).astype(BF16), window.astype(BF16), from_right(window).astype(BF16)],
            axis=0,
        )
        got = jnp.dot(w_first[:, : 3 * 64], stacked, preferred_element_type=F32)
        for b in range(6):
            u = got[b * hid : (b + 1) * hid] + bias
            at = (6 * group + b) * hid
            hidden_a[at : at + hid, :] = activated(u, start + 1 + b)

    first_layer(1)

    @pl.when(not_top)
    def _():
        to_above().wait_send()
        to_below_recv = pltpu.make_async_remote_copy(
            own, above, halo_send.at[1], halo_recv.at[0], (t, s - 1), MESH
        )
        to_below_recv.wait_recv()

    @pl.when(not_bottom)
    def _():
        to_below().wait_send()
        to_above_recv = pltpu.make_async_remote_copy(
            own, below, halo_send.at[0], halo_recv.at[1], (t, s + 1), MESH
        )
        to_above_recv.wait_recv()

    @pl.when(s == 0)
    def _():
        above[...] = jnp.zeros_like(above)

    @pl.when(s == strips - 1)
    def _():
        below[...] = jnp.zeros_like(below)

    field[:, :rows, :] = above[...].astype(F32).reshape(2 * channels, rows, cols)
    field[:, 2 * rows : 3 * rows, :] = below[...].astype(F32).reshape(2 * channels, rows, cols)
    first_layer(0)
    first_layer(2)

    source, target = hidden_a, hidden_b
    for level in range(middle):
        pairs = 8 - level
        for p in range(pairs):
            got = jnp.dot(
                w_mid[level],
                source[p * 2 * hid : p * 2 * hid + 4 * hid, :],
                preferred_element_type=F32,
            )
            u = (
                from_left(got[: 2 * hid])
                + got[2 * hid : 4 * hid]
                + from_right(got[4 * hid :])
            )
            for b in range(2):
                at = (2 * p + b) * hid
                target[at : at + hid, :] = activated(
                    u[b * hid : (b + 1) * hid], 4 + level + 2 * p + b
                )
        source, target = target, source

    count = channels * rows
    got = jnp.dot(w_last[...], source[: (rows + 2) * hid, :], preferred_element_type=F32)
    velocity = from_left(got[:count]) + got[count : 2 * count] + from_right(got[2 * count :])

    def onward(c):
        return pltpu.make_async_remote_copy(
            out_ref.at[0, c], arrived.at[c], relay_send.at[c], relay_recv.at[c], (t + 1, s), MESH
        )

    def backward(c):
        return pltpu.make_async_remote_copy(
            out_ref.at[0, c], arrived.at[c], relay_send.at[c], relay_recv.at[c], (t - 1, s), MESH
        )

    for c in range(channels):
        state = prev_ref[0, c]
        out_ref[0, c] = state + time_step * velocity[c * rows : (c + 1) * rows]

    for c in range(channels):

        @pl.when(not_first)
        def _():
            backward(c).wait_recv()
            out_ref[0, c] = out_ref[0, c] + factor_ref[t, c] * (arrived[c] - prev_ref[0, c])

        pl.when(not_last)(lambda: onward(c).start())

    @pl.when(not_last)
    def _():
        for c in range(channels):
            onward(c).wait_send()


def on_device(slices, strips, *args):
    prev, obs, bounds, factor, time_weight, win, wmid, wout = args
    channels, rows, cols = prev.shape[1:]
    hid = time_weight.shape[0]
    vmem = pl.BlockSpec(memory_space=pltpu.VMEM)
    smem = pl.BlockSpec(memory_space=pltpu.SMEM)
    return pl.pallas_call(
        functools.partial(kernel, slices, strips),
        out_shape=jax.ShapeDtypeStruct(prev.shape, F32),
        in_specs=[vmem, vmem, smem, smem, vmem, vmem, vmem, vmem],
        out_specs=vmem,
        scratch_shapes=[
            pltpu.VMEM((2 * channels * rows, cols), BF16),
            pltpu.VMEM((2 * channels * rows, cols), BF16),
            pltpu.VMEM((2 * channels * rows, cols), BF16),
            pltpu.VMEM((2 * channels, 3 * rows, cols), F32),
            pltpu.VMEM((6 * hid, 256), BF16),
            pltpu.VMEM((wmid.shape[0], 6 * hid, 4 * hid), BF16),
            pltpu.VMEM((3 * channels * rows, (rows + 2) * hid), BF16),
            pltpu.VMEM((18 * hid, cols), BF16),
            pltpu.VMEM((16 * hid, cols), BF16),
            pltpu.VMEM((channels, rows, cols), F32),
            pltpu.SemaphoreType.DMA((2,)),
            pltpu.SemaphoreType.DMA((2,)),
            pltpu.SemaphoreType.DMA((channels,)),
            pltpu.SemaphoreType.DMA((channels,)),
        ],
        compiler_params=pltpu.CompilerParams(
            collective_id=0, has_side_effects=True, vmem_limit_bytes=32 * 2**20
        ),
    )(prev, obs, bounds, factor, time_weight[None], win, wmid, wout)


def solution(mesh):
    placed = (P("tm", None, "strip", None), P(None, "strip", None), P(), P(), P(), P(), P(), P())
    return jax.shard_map(
        functools.partial(on_device, mesh.shape["tm"], mesh.shape["strip"]),
        mesh=mesh,
        in_specs=placed,
        out_specs=P("tm", None, "strip", None),
        check_vma=False,
    )
```

time: 89.9 us -> 18.8 us (0.21)
  starting transfers between devices: 42.7 us -> 0 us
  waiting for transfers between devices: 20.9 us -> 0 us
  Pallas kernels: 0 us -> 15.9 us
  matrix products: 15.7 us -> 0 us
  other arithmetic: 3.35 us -> 0 us
  between operations: 2.55 us -> 0.09 us
  local copies, waits for them, and re-layouts: 3.86 us -> 2.62 us
    ppermute x15 -> x0, starting transfers between devices: 42.7 us -> none  [the longest x6 27.4 us: extended(): lax.ppermute(lax.slice_in_dim(block, 0, width, axis=dim), axis, backward)]
    ppermute x15 -> x0, waiting for transfers between devices: 20.9 us -> none  [the longest x3 14 us: passed_along(): return lax.ppermute(shard, axis, pairs)]
    pallas_call x0 -> x1, Pallas kernels: none -> 15.9 us  [on_device(): pl.pallas_call(functools.partial(kernel, slices, strips), out_shape=jax.S...]
    dot_general x54 -> x0, matrix products: 15.7 us -> none  [convolve(): jnp.einsum('oc,crw->orw', weight[shift_row, shift_col], window, preferred...]
    concatenate x6 -> x0, other arithmetic: 1.68 us -> none  [extended(): block = jnp.concatenate([low, block, high], axis=dim)]
    dynamic_slice x1 -> x0, local copies, waits for them, and re-layouts: 1.39 us -> none  [on_device(): lax.dynamic_index_in_dim(bounds, slice_index + 1, 0, keepdims=False)]
    mul x2 -> x0, other arithmetic: 1.35 us -> none  [the longest x1 0.69 us: on_device(): jump = fine - keeper * factor[:, None, None] * start_state]
    unnamed x10 -> x16, local copies, waits for them, and re-layouts: 1.74 us -> 2.62 us
  transfers between devices with their start and end apart: 15 -> 0, of which waited for: 7 -> 0; matrix products, arithmetic and copies ran while one was open for 3% -> 0% of each run, Pallas kernels for 0% -> 0%
where the time goes in v1:
time: 18.8 us; the launch traced here: 18.6 us
  Pallas kernels  15.9 us (85%)
  local copies, waits for them, and re-layouts  2.62 us (14%)
    pallas_call x1, Pallas kernels, on_device(): pl.pallas_call(functools.partial(kernel, slices, strips), out_shape=jax.S...  15.9 us
    unnamed x16, local copies, waits for them, and re-layouts  2.62 us

profile of v1, /device:TPU:28, one launch (start us, length us, event | category | flops | bytes accessed | tf_op | source)
XLA Modules:
  0.0 18.6 jit_solution(8291874242430852029)
XLA Ops:
  0.0 0.0 copy-start.1
  0.0 0.0 copy-start.2
  0.0 0.0 copy-start.3
  0.0 0.0 copy-start.4
  0.0 0.0 copy-start.5
  0.0 0.0 copy-start.6
  0.0 0.9 %copy.9.win_ref = bf16[3,3,64,8]{3,2,1,0:T(8,128)(2,1)S(1)} copy(bf16[3,3,64,8]{2,3,1,0:T(8,128)(2,1)} %param.13) | data formatting | bytes 18432 | tf_op args[5]
  1.0 0.0 copy-done.1
  1.0 0.0 copy-done.2
  1.0 0.0 copy-done.3
  1.0 0.0 copy-done.4
  1.0 0.0 copy-done.5
  1.0 0.0 copy-done.6
  1.0 0.0 copy-start
  1.0 1.1 %copy-done = bf16[4,3,3,64,64]{4,3,2,1,0:T(8,128)(2,1)S(1)} copy-done((bf16[4,3,3,64,64]{4,3,2,1,0:T(8,128)(2,1)S(1)}, bf16[4,3,3,64,64]{4,3,2,1,0:T(8,128)(2,1)}, u32[]{:S(2)}) %copy-start) | copy-done | bytes 294936
  2.1 15.9 %shard_map.82 = f32[1,4,8,384]{3,2,1,0:T(8,128)S(1)} custom-call(f32[1,4,8,384]{3,2,1,0:T(8,128)S(1)} %copy-done.1, bf16[4,8,384]{2,1,0:T(8,128)(2,1)S(1)} %copy-done.2, s32[5]{0:T(128)S(1)} %copy-done.5, f32[4,4]{1,0:T(4,128)S(1)} %copy-done.4, f32[1,64]{1,0:T(1,128)S(1)} %bitcast.1, bf16[3,3,64,8]{3,2,1,0:T(8,128)(2,1)S(1)} %copy.9.win_ref, ...), custom_call_target="tpu_custom_call" | custom-call | tf_op jit(solution)/shard_map/pallas_call | solution.py:262
  18.0 0.6 %copy.11 = f32[1,4,8,384]{3,2,1,0:T(8,128)} copy(f32[1,4,8,384]{3,2,1,0:T(8,128)S(1)} %shard_map.82) | data formatting | bytes 98304
Async XLA Ops:
  0.0 1.0 %copy-start.1 = (f32[1,4,8,384]{3,2,1,0:T(8,128)S(1)}, f32[1,4,8,384]{3,2,1,0:T(8,128)}, u32[]{:S(2)}) copy-start(f32[1,4,8,384]{3,2,1,0:T(8,128)} %prev_ref.1) | copy-start | bytes 147460
  0.0 1.0 %copy-start.2 = (bf16[4,8,384]{2,1,0:T(8,128)(2,1)S(1)}, bf16[4,8,384]{2,1,0:T(8,128)(2,1)}, u32[]{:S(2)}) copy-start(bf16[4,8,384]{2,1,0:T(8,128)(2,1)} %obs_ref.1) | copy-start | bytes 73732
  0.0 1.0 %copy-start.3 = (bf16[3,3,4,64]{3,2,1,0:T(4,128)(2,1)S(1)}, bf16[3,3,4,64]{3,2,1,0:T(4,128)(2,1)}, u32[]{:S(2)}) copy-start(bf16[3,3,4,64]{3,2,1,0:T(4,128)(2,1)} %wout_ref.1) | copy-start | bytes 13828
  0.0 1.0 %copy-start.4 = (f32[4,4]{1,0:T(4,128)S(1)}, f32[4,4]{1,0:T(4,128)}, u32[]{:S(2)}) copy-start(f32[4,4]{1,0:T(4,128)} %factor_ref.1) | copy-start | bytes 196
  0.0 1.0 %copy-start.5 = (s32[5]{0:T(128)S(1)}, s32[5]{0:T(128)}, u32[]{:S(2)}) copy-start(s32[5]{0:T(128)} %bounds_ref.1) | copy-start | bytes 64
  0.0 1.0 %copy-start.6 = (f32[64]{0:T(128)S(1)}, f32[64]{0:T(128)}, u32[]{:S(2)}) copy-start(f32[64]{0:T(128)} %param.12) | copy-start | bytes 772
  1.0 1.1 %copy-start = (bf16[4,3,3,64,64]{4,3,2,1,0:T(8,128)(2,1)S(1)}, bf16[4,3,3,64,64]{4,3,2,1,0:T(8,128)(2,1)}, u32[]{:S(2)}) copy-start(bf16[4,3,3,64,64]{4,3,2,1,0:T(8,128)(2,1)} %wmid_ref.1) | copy-start | bytes 884740

commit v2 on v1

--- a/solution.py
+++ b/solution.py
@@ -16,30 +16,34 @@
 def kernel(
     slices,
     strips,
-    prev_ref,
-    obs_ref,
-    bounds_ref,
-    factor_ref,
-    time_ref,
-    win_ref,
-    wmid_ref,
-    wout_ref,
-    out_ref,
-    own,
-    above,
-    below,
-    field,
-    w_first,
-    w_mid,
-    w_last,
-    hidden_a,
-    hidden_b,
-    arrived,
-    halo_send,
-    halo_recv,
-    relay_send,
-    relay_recv,
+    *refs,
 ):
+    operands, (out_ref, *local), refs = refs[:8], refs[8:17], refs[17:]
+    prev_ref, obs_ref, bounds_ref, factor_ref, time_ref, win_ref, wmid_ref, wout_ref = local
+    (
+        load_sem,
+        own,
+        above,
+        below,
+        field,
+        w_first,
+        w_mid,
+        w_last,
+        hidden_a,
+        hidden_b,
+        arrived,
+        halo_send,
+        halo_recv,
+        relay_send,
+        relay_recv,
+    ) = refs
+
+    loads = [
+        pltpu.make_async_copy(source, place, load_sem.at[k])
+        for k, (source, place) in enumerate(zip(operands, local))
+    ]
+    for load in loads:
+        load.start()
     t = lax.axis_index("tm")
     s = lax.axis_index("strip")
     channels, rows, cols = prev_ref.shape[1:]
@@ -58,6 +62,8 @@
     pl.when(not_first)(lambda: greet(t - 1, s))
     pl.when(not_last)(lambda: greet(t + 1, s))
 
+    loads[0].wait()
+    loads[1].wait()
     for c in range(channels):
         field[c, rows : 2 * rows, :] = prev_ref[0, c]
         field[channels + c, rows : 2 * rows, :] = obs_ref[c].astype(F32)
@@ -84,13 +90,17 @@
     pl.when(not_top)(lambda: to_above().start())
     pl.when(not_bottom)(lambda: to_below().start())
 
+    for load in loads[2:]:
+        load.wait()
     lane = lax.broadcasted_iota(jnp.int32, (2 * channels, 256), 1)
     chan = lax.broadcasted_iota(jnp.int32, (2 * channels, 256), 0)
     base = jnp.zeros((hid, 256), F32)
     for i in range(3):
         for j in range(3):
             pick = (lane == j * 64 + chan * 8 + i).astype(F32).astype(BF16)
-            base = base + jnp.dot(win_ref[i, j], pick, preferred_element_type=F32)
+            base = base + lax.dot_general(
+                win_ref[i, j], pick, (((0,), (0,)), ((), ())), preferred_element_type=F32
+            )
     base = base * 0.5
     for b in range(6):
         turned = pltpu.roll(base, b, 1) if b else base
@@ -257,14 +267,20 @@
     prev, obs, bounds, factor, time_weight, win, wmid, wout = args
     channels, rows, cols = prev.shape[1:]
     hid = time_weight.shape[0]
-    vmem = pl.BlockSpec(memory_space=pltpu.VMEM)
-    smem = pl.BlockSpec(memory_space=pltpu.SMEM)
+    operands = (prev, obs, bounds, factor, time_weight[None])
+    operands += (win.transpose(0, 1, 3, 2), wmid, wout)
+    local = [
+        (pltpu.SMEM if a is bounds or a is factor else pltpu.VMEM)(a.shape, a.dtype)
+        for a in operands
+    ]
     return pl.pallas_call(
         functools.partial(kernel, slices, strips),
         out_shape=jax.ShapeDtypeStruct(prev.shape, F32),
-        in_specs=[vmem, vmem, smem, smem, vmem, vmem, vmem, vmem],
-        out_specs=vmem,
+        in_specs=[pl.BlockSpec(memory_space=pltpu.HBM)] * len(operands),
+        out_specs=pl.BlockSpec(memory_space=pltpu.VMEM),
         scratch_shapes=[
+            *local,
+            pltpu.SemaphoreType.DMA((len(operands),)),
             pltpu.VMEM((2 * channels * rows, cols), BF16),
             pltpu.VMEM((2 * channels * rows, cols), BF16),
             pltpu.VMEM((2 * channels * rows, cols), BF16),
@@ -281,9 +297,9 @@
             pltpu.SemaphoreType.DMA((channels,)),
         ],
         compiler_params=pltpu.CompilerParams(
-            collective_id=0, has_side_effects=True, vmem_limit_bytes=32 * 2**20
+            collective_id=0, has_side_effects=True, vmem_limit_bytes=60 * 2**20
         ),
-    )(prev, obs, bounds, factor, time_weight[None], win, wmid, wout)
+    )(*operands)
 
 
 def solution(mesh):

time: 18.8 us -> 17.6 us (0.936)
  local copies, waits for them, and re-layouts: 2.62 us -> 1.42 us
    unnamed x16 -> x1, local copies, waits for them, and re-layouts: 2.62 us -> 1.42 us
where the time goes in v2:
time: 17.6 us; the launch traced here: 17.4 us
  Pallas kernels  16 us (91%)
  local copies, waits for them, and re-layouts  1.42 us (8%)
    pallas_call x1, Pallas kernels, on_device(): pl.pallas_call(functools.partial(kernel, slices, strips), out_shape=jax.S...  16 us
    unnamed x1, local copies, waits for them, and re-layouts  1.42 us

profile of v2, /device:TPU:28, one launch (start us, length us, event | category | flops | bytes accessed | tf_op | source)
XLA Modules:
  0.0 17.4 jit_solution(172657181466232257)
XLA Ops:
  0.0 16.0 %shard_map.82 = f32[1,4,8,384]{3,2,1,0:T(8,128)} custom-call(f32[1,4,8,384]{3,2,1,0:T(8,128)} %refs_0_.1, bf16[4,8,384]{2,1,0:T(8,128)(2,1)} %refs_1_.1, s32[5]{0:T(128)} %refs_2_.1, f32[4,4]{1,0:T(4,128)} %refs_3_.1, f32[1,64]{1,0:T(1,128)} %bitcast.3, bf16[3,3,8,64]{3,2,1,0:T(8,128)(2,1)} %bitcast.2, bf16[4,3,3,64,64]{4,3,2,1,0:T(8,128)(2,1)} %refs_6_.1, ...), custom_call_target="tpu_custom_call" | custom-call | tf_op jit(solution)/shard_map/pallas_call | solution.py:276
  16.0 1.4 %copy.10 = f32[1,4,8,384]{3,2,1,0:T(8,128)} copy(f32[1,4,8,384]{3,2,1,0:T(8,128)} %shard_map.82) | data formatting | bytes 98304

commit v3 on v2

--- a/solution.py
+++ b/solution.py
@@ -31,11 +31,15 @@
         w_last,
         hidden_a,
         hidden_b,
-        arrived,
+        speed,
+        states,
+        speeds,
         halo_send,
         halo_recv,
-        relay_send,
-        relay_recv,
+        state_send,
+        state_recv,
+        speed_send,
+        speed_recv,
     ) = refs
 
     loads = [
@@ -50,7 +54,6 @@
     hid = time_ref.shape[1]
     middle = wmid_ref.shape[0]
     not_top, not_bottom = s > 0, s < strips - 1
-    not_first, not_last = t > 0, t < slices - 1
 
     barrier = pltpu.get_barrier_semaphore()
 
@@ -59,8 +62,8 @@
 
     pl.when(not_top)(lambda: greet(t, s - 1))
     pl.when(not_bottom)(lambda: greet(t, s + 1))
-    pl.when(not_first)(lambda: greet(t - 1, s))
-    pl.when(not_last)(lambda: greet(t + 1, s))
+    for k in range(1, slices):
+        greet(lax.rem(t + k, slices), s)
 
     loads[0].wait()
     loads[1].wait()
@@ -70,10 +73,7 @@
     own[...] = field[:, rows : 2 * rows, :].reshape(2 * channels * rows, cols).astype(BF16)
 
     greeted = (
-        not_top.astype(jnp.int32)
-        + not_bottom.astype(jnp.int32)
-        + not_first.astype(jnp.int32)
-        + not_last.astype(jnp.int32)
+        not_top.astype(jnp.int32) + not_bottom.astype(jnp.int32) + (slices - 1)
     )
     pl.semaphore_wait(barrier, greeted)
 
@@ -89,6 +89,19 @@
 
     pl.when(not_top)(lambda: to_above().start())
     pl.when(not_bottom)(lambda: to_below().start())
+
+    def state_copy(k, to):
+        return pltpu.make_async_remote_copy(
+            prev_ref, states.at[k - 1], state_send.at[k - 1], state_recv.at[k - 1], (to, s), MESH
+        )
+
+    def speed_copy(k, to):
+        return pltpu.make_async_remote_copy(
+            speed, speeds.at[k - 1], speed_send.at[k - 1], speed_recv.at[k - 1], (to, s), MESH
+        )
+
+    for k in reversed(range(1, slices)):
+        pl.when(t + k < slices)(lambda: state_copy(k, t + k).start())
 
     for load in loads[2:]:
         load.wait()
@@ -234,33 +247,49 @@
     got = jnp.dot(w_last[...], source[: (rows + 2) * hid, :], preferred_element_type=F32)
     velocity = from_left(got[:count]) + got[count : 2 * count] + from_right(got[2 * count :])
 
-    def onward(c):
-        return pltpu.make_async_remote_copy(
-            out_ref.at[0, c], arrived.at[c], relay_send.at[c], relay_recv.at[c], (t + 1, s), MESH
-        )
-
-    def backward(c):
-        return pltpu.make_async_remote_copy(
-            out_ref.at[0, c], arrived.at[c], relay_send.at[c], relay_recv.at[c], (t - 1, s), MESH
-        )
-
+    speed[...] = velocity.astype(BF16)
+    for k in reversed(range(1, slices)):
+        pl.when(t + k < slices)(lambda: speed_copy(k, t + k).start())
+
+    keep = (t > 0).astype(F32)
     for c in range(channels):
-        state = prev_ref[0, c]
-        out_ref[0, c] = state + time_step * velocity[c * rows : (c + 1) * rows]
-
-    for c in range(channels):
-
-        @pl.when(not_first)
+        moved = time_step * velocity[c * rows : (c + 1) * rows]
+        out_ref[0, c] = (1.0 - keep * factor_ref[t, c]) * prev_ref[0, c] + moved
+
+    def decay(k, c):
+        product = factor_ref[t, c]
+        for back in range(1, k):
+            product = product * factor_ref[jnp.maximum(t - back, 0), c]
+        return product
+
+    for k in range(1, slices):
+
+        @pl.when(t >= k)
         def _():
-            backward(c).wait_recv()
-            out_ref[0, c] = out_ref[0, c] + factor_ref[t, c] * (arrived[c] - prev_ref[0, c])
-
-        pl.when(not_last)(lambda: onward(c).start())
-
-    @pl.when(not_last)
-    def _():
-        for c in range(channels):
-            onward(c).wait_send()
+            state_copy(k, t - k).wait_recv()
+            keep = (t > k).astype(F32)
+            for c in range(channels):
+                scale = decay(k, c) * (1.0 - keep * factor_ref[jnp.maximum(t - k, 0), c])
+                out_ref[0, c] = out_ref[0, c] + scale * states[k - 1, 0, c]
+
+    for k in range(1, slices):
+
+        @pl.when(t >= k)
+        def _():
+            origin = jnp.maximum(t - k, 0)
+            step = (bounds_ref[origin + 1] - bounds_ref[origin]).astype(F32) / STEPS
+            speed_copy(k, t - k).wait_recv()
+            taken = speeds[k - 1].astype(F32)
+            for c in range(channels):
+                part = taken[c * rows : (c + 1) * rows]
+                out_ref[0, c] = out_ref[0, c] + (decay(k, c) * step) * part
+
+    for k in range(1, slices):
+
+        @pl.when(t + k < slices)
+        def _():
+            state_copy(k, t + k).wait_send()
+            speed_copy(k, t + k).wait_send()
 
 
 def on_device(slices, strips, *args):
@@ -290,11 +319,15 @@
             pltpu.VMEM((3 * channels * rows, (rows + 2) * hid), BF16),
             pltpu.VMEM((18 * hid, cols), BF16),
             pltpu.VMEM((16 * hid, cols), BF16),
-            pltpu.VMEM((channels, rows, cols), F32),
+            pltpu.VMEM((channels * rows, cols), BF16),
+            pltpu.VMEM((slices - 1, *prev.shape), F32),
+            pltpu.VMEM((slices - 1, channels * rows, cols), BF16),
             pltpu.SemaphoreType.DMA((2,)),
             pltpu.SemaphoreType.DMA((2,)),
-            pltpu.SemaphoreType.DMA((channels,)),
-            pltpu.SemaphoreType.DMA((channels,)),
+            pltpu.SemaphoreType.DMA((slices - 1,)),
+            pltpu.SemaphoreType.DMA((slices - 1,)),
+            pltpu.SemaphoreType.DMA((slices - 1,)),
+            pltpu.SemaphoreType.DMA((slices - 1,)),
         ],
         compiler_params=pltpu.CompilerParams(
             collective_id=0, has_side_effects=True, vmem_limit_bytes=60 * 2**20

time: 17.6 us -> 15.6 us (0.89)
  the two profiles are of different devices: /device:TPU:28 before, /device:TPU:13 now
where the time goes in v3:
time: 15.6 us; the launch traced here: 15.4 us
  Pallas kernels  14 us (90%)
  local copies, waits for them, and re-layouts  1.42 us (9%)
    pallas_call x1, Pallas kernels, on_device(): pl.pallas_call(functools.partial(kernel, slices, strips), out_shape=jax.S...  14 us
    unnamed x1, local copies, waits for them, and re-layouts  1.42 us

profile of v3, /device:TPU:13, one launch (start us, length us, event | category | flops | bytes accessed | tf_op | source)
XLA Modules:
  0.0 15.4 jit_solution(3249589329932203295)
XLA Ops:
  0.0 14.0 %shard_map.82 = f32[1,4,8,384]{3,2,1,0:T(8,128)} custom-call(f32[1,4,8,384]{3,2,1,0:T(8,128)} %refs_0_.1, bf16[4,8,384]{2,1,0:T(8,128)(2,1)} %refs_1_.1, s32[5]{0:T(128)} %refs_2_.1, f32[4,4]{1,0:T(4,128)} %refs_3_.1, f32[1,64]{1,0:T(1,128)} %bitcast.3, bf16[3,3,8,64]{3,2,1,0:T(8,128)(2,1)} %bitcast.2, bf16[4,3,3,64,64]{4,3,2,1,0:T(8,128)(2,1)} %refs_6_.1, ...), custom_call_target="tpu_custom_call" | custom-call | tf_op jit(solution)/shard_map/pallas_call | solution.py:305
  14.0 1.4 %copy.10 = f32[1,4,8,384]{3,2,1,0:T(8,128)} copy(f32[1,4,8,384]{3,2,1,0:T(8,128)} %shard_map.82) | data formatting | bytes 98304

commit v4 on v3

--- a/solution.py
+++ b/solution.py
@@ -191,7 +191,21 @@
             at = (6 * group + b) * hid
             hidden_a[at : at + hid, :] = activated(u, start + 1 + b)
 
+    def middle_pair(level, p, source, target):
+        got = jnp.dot(
+            w_mid[level],
+            source[p * 2 * hid : p * 2 * hid + 4 * hid, :],
+            preferred_element_type=F32,
+        )
+        u = from_left(got[: 2 * hid]) + got[2 * hid : 4 * hid] + from_right(got[4 * hid :])
+        for b in range(2):
+            at = (2 * p + b) * hid
+            target[at : at + hid, :] = activated(u[b * hid : (b + 1) * hid], 4 + level + 2 * p + b)
+
     first_layer(1)
+    inner = (3, 4)
+    for p in inner:
+        middle_pair(0, p, hidden_a, hidden_b)
 
     @pl.when(not_top)
     def _():
@@ -224,23 +238,9 @@
 
     source, target = hidden_a, hidden_b
     for level in range(middle):
-        pairs = 8 - level
-        for p in range(pairs):
-            got = jnp.dot(
-                w_mid[level],
-                source[p * 2 * hid : p * 2 * hid + 4 * hid, :],
-                preferred_element_type=F32,
-            )
-            u = (
-                from_left(got[: 2 * hid])
-                + got[2 * hid : 4 * hid]
-                + from_right(got[4 * hid :])
-            )
-            for b in range(2):
-                at = (2 * p + b) * hid
-                target[at : at + hid, :] = activated(
-                    u[b * hid : (b + 1) * hid], 4 + level + 2 * p + b
-                )
+        for p in range(8 - level):
+            if level or p not in inner:
+                middle_pair(level, p, source, target)
         source, target = target, source
 
     count = channels * rows

time: 15.6 us -> 15.4 us (0.987)
  Pallas kernels: 14 us -> 13.8 us
    pallas_call x1, Pallas kernels: 14 us -> 13.8 us  [on_device(): pl.pallas_call(functools.partial(kernel, slices, strips), out_shape=jax.S...]
where the time goes in v4:
time: 15.4 us; the launch traced here: 15.2 us
  Pallas kernels  13.8 us (90%)
  local copies, waits for them, and re-layouts  1.42 us (9%)
    pallas_call x1, Pallas kernels, on_device(): pl.pallas_call(functools.partial(kernel, slices, strips), out_shape=jax.S...  13.8 us
    unnamed x1, local copies, waits for them, and re-layouts  1.42 us

profile of v4, /device:TPU:13, one launch (start us, length us, event | category | flops | bytes accessed | tf_op | source)
XLA Modules:
  0.0 15.2 jit_solution(4664453527414111847)
XLA Ops:
  0.0 13.8 %shard_map.82 = f32[1,4,8,384]{3,2,1,0:T(8,128)} custom-call(f32[1,4,8,384]{3,2,1,0:T(8,128)} %refs_0_.1, bf16[4,8,384]{2,1,0:T(8,128)(2,1)} %refs_1_.1, s32[5]{0:T(128)} %refs_2_.1, f32[4,4]{1,0:T(4,128)} %refs_3_.1, f32[1,64]{1,0:T(1,128)} %bitcast.3, bf16[3,3,8,64]{3,2,1,0:T(8,128)(2,1)} %bitcast.2, bf16[4,3,3,64,64]{4,3,2,1,0:T(8,128)(2,1)} %refs_6_.1, ...), custom_call_target="tpu_custom_call" | custom-call | tf_op jit(solution)/shard_map/pallas_call | solution.py:305
  13.8 1.4 %copy.10 = f32[1,4,8,384]{3,2,1,0:T(8,128)} copy(f32[1,4,8,384]{3,2,1,0:T(8,128)} %shard_map.82) | data formatting | bytes 98304
